TPU v7x, 256 devices: a whole 4x4x8 slice. The times are simulated.
256 devices in a mesh: row: 8 (over x, core), col: 32 (over z, y).
Axes of the slice: x: 4, y: 4, z: 8, core: 2. Of those that a mesh axis runs over, the one named last changes fastest.
Arguments:
- right_sides: float32 [4, 8, 32, 128, 128], P(None, 'row', 'col'), may hold values from -6 to 6
- inverses: bfloat16 [4, 8, 32, 128, 128], P(None, 'row', 'col'), may hold values from -1 to 2, as said below
- blocks: bfloat16 [3, 8, 32, 2, 8, 6, 128, 128], P(None, 'row', 'col'), may hold values from -0.0546875 to 0.0546875
- sources: int32 [3, 8, 32, 2, 8, 6], P(None, 'row', 'col'), may hold values from 0 to 31
Outputs:
- solution: bfloat16 [4, 8, 32, 128, 128], P(None, 'row', 'col')
- back_solution: float32 [4, 8, 32, 128, 128], P(None, 'row', 'col')
Inputs may be any that keep to these rules, and one draw needn't show every extreme that they name: `inverses`: each matrix is the inverse of one supernode's diagonal block.
All inputs are finite; a program needn't handle non-finite values.
Results may differ from a plain program's by a relative error of at most 0.03.
Values may be sent and summed in bfloat16 or wider, within the bound.
A program may use at most 64 MiB of HBM per device.

v0:
```python
import jax
import jax.numpy as jnp
from jax import lax
from jax.sharding import PartitionSpec as P


def forward_terms(blocks, sources, column_level, jump_index, gathered):
    chosen = jnp.take(gathered, sources[column_level, jump_index], axis=0)
    return jnp.einsum(
        "tkab,tkbs->tas",
        blocks[column_level, jump_index],
        chosen,
        preferred_element_type=jnp.float32,
    )


def backward_terms(blocks, sources, column_level, jump_index, column_copy, grid_cols):
    products = jnp.einsum(
        "tkab,tas->tkbs",
        blocks[column_level, jump_index],
        column_copy,
        preferred_element_type=jnp.float32,
    )
    flattened = products.reshape(-1, products.shape[2] * products.shape[3])
    chosen = sources[column_level, jump_index].reshape(-1)
    onehot = (chosen[None, :] == jnp.arange(grid_cols, dtype=jnp.int32)[:, None]).astype(
        jnp.float32
    )
    summed = jnp.dot(
        onehot, flattened, precision=lax.Precision.HIGHEST, preferred_element_type=jnp.float32
    )
    return summed.reshape(grid_cols, products.shape[2], products.shape[3])


def reduce_rows(pending_sum):
    return lax.psum_scatter(
        pending_sum.astype(jnp.bfloat16), "row", scatter_dimension=0, tiled=True
    ).astype(jnp.float32)[0]


def gather_column(back_value):
    return lax.all_gather(back_value.astype(jnp.bfloat16)[None], "row", axis=0, tiled=True)


def body(right_sides, inverses, blocks, sources):
    right_sides = right_sides[:, 0, 0]
    inverses = inverses[:, 0, 0]
    blocks = blocks[:, 0, 0]
    sources = sources[:, 0, 0]
    levels = right_sides.shape[0]
    summit = levels - 1
    grid_rows = lax.axis_size("row")
    grid_cols = lax.axis_size("col")
    block_rows = right_sides.shape[1]
    rhs_count = right_sides.shape[2]
    pending = [
        jnp.zeros((grid_rows, block_rows, rhs_count), jnp.float32) for height in range(levels)
    ]
    solved_list = []
    for height in range(summit):
        if height > 0:
            update = reduce_rows(pending[height])
            forward_rhs = (right_sides[height] - update).astype(jnp.bfloat16)
        else:
            forward_rhs = right_sides[height].astype(jnp.bfloat16)
        solved = jnp.dot(inverses[height], forward_rhs, preferred_element_type=jnp.float32).astype(
            jnp.bfloat16
        )
        solved_list.append(solved)
        gathered = lax.all_gather(solved[None], "col", axis=0, tiled=True)
        for jump_index in range(2):
            target = min(height + 1 + jump_index, summit)
            pending[target] = pending[target] + forward_terms(
                blocks, sources, height, jump_index, gathered
            )
    update = reduce_rows(pending[summit])
    forward_rhs = (right_sides[summit] - update).astype(jnp.bfloat16)
    top_solved = jnp.dot(inverses[summit], forward_rhs, preferred_element_type=jnp.float32).astype(
        jnp.bfloat16
    )
    top_back = jnp.einsum(
        "ba,bs->as", inverses[summit], top_solved, preferred_element_type=jnp.float32
    )
    top_copy = gather_column(top_back)
    solved_list.append(top_solved)
    copies = [None] * levels
    back_values = [None] * levels
    copies[summit] = top_copy
    back_values[summit] = top_back
    for height in range(summit - 1, -1, -1):
        far_part = backward_terms(
            blocks, sources, height, 1, copies[min(height + 2, summit)], grid_cols
        )
        near_part = backward_terms(blocks, sources, height, 0, copies[height + 1], grid_cols)
        back_update = lax.psum_scatter(
            (near_part + far_part).astype(jnp.bfloat16), "col", scatter_dimension=0, tiled=True
        ).astype(jnp.float32)[0]
        back_rhs = (solved_list[height].astype(jnp.float32) - back_update).astype(jnp.bfloat16)
        back_value = jnp.einsum(
            "ba,bs->as", inverses[height], back_rhs, preferred_element_type=jnp.float32
        )
        back_values[height] = back_value
        if height > 0:
            copies[height] = gather_column(back_value)
    return (jnp.stack(solved_list)[:, None, None], jnp.stack(back_values)[:, None, None])


def solution(mesh):
    return jax.shard_map(
        body,
        mesh=mesh,
        in_specs=(
            P(None, "row", "col", None, None),
            P(None, "row", "col", None, None),
            P(None, "row", "col", None, None, None, None, None),
            P(None, "row", "col", None, None, None),
        ),
        out_specs=(P(None, "row", "col", None, None), P(None, "row", "col", None, None)),
        check_vma=False,
    )
```

profile of v0, /device:TPU:1, one launch (start us, length us, event | category | flops | bytes accessed | tf_op | source)
XLA Modules:
  0.0 1094.8 jit_solution(11607165707230820834)
XLA Ops:
  7.2 1.6 convolution_convert_fusion.3
  8.9 0.8 copy.34
  9.8 77.0 %all-gather.10.cloned.1.call-done = bf16[4096,128]{1,0:T(8,128)(2,1)} async-done(((bf16[128,128]{1,0:T(8,128)(2,1)}), bf16[4096,128]{1,0:T(8,128)(2,1)}) %all-gather.10.cloned.1.call-update) | async-done | bytes 1048592 | tf_op jit(solution)/shard_map/all_gather | solution.py:70
  86.8 2.1 gather_fusion
  88.9 0.9 copy.35
  89.8 2.8 fusion.81
  92.9 32.8 %reduce-scatter.7.cloned.1.call-done = bf16[1,128,128]{1,2,0:T(8,128)(2,1)} async-done(((bf16[8,128,128]{1,2,0:T(8,128)(2,1)}), bf16[1,128,128]{1,2,0:T(8,128)(2,1)}) %reduce-scatter.7.cloned.1.call-update) | async-done | bytes 32784 | tf_op jit(solution)/shard_map/reduce_scatter | solution.py:36
  125.6 1.5 convolution_convert_fusion.2
  127.4 0.8 gather_fusion.1
  128.3 1.6 copy.38
  129.9 3.3 fusion.42
  133.2 68.4 %all-gather.12.cloned.1.call-done = bf16[4096,128]{1,0:T(8,128)(2,1)} async-done(((bf16[128,128]{1,0:T(8,128)(2,1)}), bf16[4096,128]{1,0:T(8,128)(2,1)}) %all-gather.12.cloned.1.call-update) | async-done | bytes 1048592 | tf_op jit(solution)/shard_map/all_gather | solution.py:70
  201.6 2.1 gather_fusion.2
  203.6 0.9 copy.39
  204.6 2.9 fusion.78
  207.7 32.8 %reduce-scatter.9.cloned.1.call-done = bf16[1,128,128]{1,2,0:T(8,128)(2,1)} async-done(((bf16[8,128,128]{1,2,0:T(8,128)(2,1)}), bf16[1,128,128]{1,2,0:T(8,128)(2,1)}) %reduce-scatter.9.cloned.1.call-update) | async-done | bytes 32784 | tf_op jit(solution)/shard_map/reduce_scatter | solution.py:36
  240.4 1.5 convolution_convert_fusion.1
  242.3 0.8 gather_fusion.3
  243.2 1.6 copy.42
  244.8 2.5 fusion.48
  247.3 68.6 %all-gather.14.cloned.1.call-done = bf16[4096,128]{1,0:T(8,128)(2,1)} async-done(((bf16[128,128]{1,0:T(8,128)(2,1)}), bf16[4096,128]{1,0:T(8,128)(2,1)}) %all-gather.14.cloned.1.call-update) | async-done | bytes 1048592 | tf_op jit(solution)/shard_map/all_gather | solution.py:70
  315.9 2.1 gather_fusion.4
  318.0 1.6 copy.43
  319.6 0.8 gather_fusion.5
  320.4 1.6 copy.44
  322.0 2.6 fusion.60
  324.6 2.8 fusion.75
  327.6 0.6 eq.102
  328.8 31.6 %reduce-scatter.11.cloned.1.call-done = bf16[1,128,128]{1,2,0:T(8,128)(2,1)} async-done(((bf16[8,128,128]{1,2,0:T(8,128)(2,1)}), bf16[1,128,128]{1,2,0:T(8,128)(2,1)}) %reduce-scatter.11.cloned.1.call-update) | async-done | bytes 32784 | tf_op jit(solution)/shard_map/reduce_scatter | solution.py:36
  360.4 0.9 convolution_convert_fusion
  361.3 0.8 bitcast_convert_fusion.2
  362.1 14.7 %all-gather.3 = bf16[1024,128]{0,1:T(8,128)(2,1)S(1)} all-gather(bf16[128,128]{0,1:T(8,128)(2,1)S(1)} %get-tuple-element.28), channel_id=5, replica_groups=mesh['row'=8,'col'=32] {'row'}, dimensions={0}, use_global_device_ids=true | all-gather | bytes 294912 | tf_op jit(solution)/shard_map/all_gather | solution.py:42
  376.9 3.7 convolution_bitcast_fusion.4
  380.5 2.0 convolution_bitcast_fusion.5
  382.5 3.5 copy.50
  386.0 2.4 copy.47
  388.4 5.2 fusion.12
  393.6 3.3 fusion.15
  396.9 3.3 fusion.20
  400.4 0.6 eq.94
  401.1 2.0 convolution_bitcast_fusion.2
  403.1 2.3 copy.58
  405.4 6.3 fusion.6
  411.7 198.1 %reduce-scatter.13.cloned.1.call-done = bf16[1,128,128]{2,1,0:T(8,128)(2,1)} async-done(((bf16[32,128,128]{2,1,0:T(8,128)(2,1)}), bf16[1,128,128]{2,1,0:T(8,128)(2,1)}) %reduce-scatter.13.cloned.1.call-update) | async-done | bytes 32784 | tf_op jit(solution)/shard_map/reduce_scatter | solution.py:95
  609.8 1.6 bitcast_convert_fusion.1
  611.4 17.8 %all-gather.4 = bf16[1024,128]{0,1:T(8,128)(2,1)S(1)} all-gather(bf16[128,128]{0,1:T(8,128)(2,1)S(1)} %get-tuple-element.30), channel_id=6, replica_groups=mesh['row'=8,'col'=32] {'row'}, dimensions={0}, use_global_device_ids=true | all-gather | bytes 294912 | tf_op jit(solution)/shard_map/all_gather | solution.py:42
  629.2 2.0 convolution_bitcast_fusion.3
  631.2 2.3 copy.55
  633.6 5.1 fusion.9
  638.7 3.3 fusion.19
  642.5 2.0 convolution_bitcast_fusion
  644.4 2.3 copy.66
  646.8 6.3 fusion
  653.1 195.2 %reduce-scatter.15.cloned.1.call-done = bf16[1,128,128]{2,1,0:T(8,128)(2,1)} async-done(((bf16[32,128,128]{2,1,0:T(8,128)(2,1)}), bf16[1,128,128]{2,1,0:T(8,128)(2,1)}) %reduce-scatter.15.cloned.1.call-update) | async-done | bytes 32784 | tf_op jit(solution)/shard_map/reduce_scatter | solution.py:95
  848.3 0.9 bitcast_convert_fusion
  849.3 17.9 %all-gather.5 = bf16[1024,128]{0,1:T(8,128)(2,1)S(1)} all-gather(bf16[128,128]{0,1:T(8,128)(2,1)S(1)} %get-tuple-element.32), channel_id=7, replica_groups=mesh['row'=8,'col'=32] {'row'}, dimensions={0}, use_global_device_ids=true | all-gather | bytes 294912 | tf_op jit(solution)/shard_map/all_gather | solution.py:42
  867.2 2.0 convolution_bitcast_fusion.1
  869.2 2.3 copy.63
  871.5 5.1 fusion.3
  876.7 3.3 fusion.18
  880.1 0.7 maximum_bitcast_fusion.1
  880.7 205.5 %reduce-scatter.17.cloned.1.call-done = bf16[1,128,128]{2,1,0:T(8,128)(2,1)} async-done(((bf16[32,128,128]{2,1,0:T(8,128)(2,1)}), bf16[1,128,128]{2,1,0:T(8,128)(2,1)}) %reduce-scatter.17.cloned.1.call-update) | async-done | bytes 32784 | tf_op jit(solution)/shard_map/reduce_scatter | solution.py:95
  1086.3 0.9 convolution_bitcast_fusion.6
  1087.2 0.8 copy.71
  (83 shorter events, 2.8 us)
Async XLA Ops:
  7.2 79.6 %all-gather.10.cloned.1.call-start = ((), (), s32[]{:S(2)}) async-start(), calls=%async_computation.12 | async-start | bytes 1081344 | tf_op jit(solution)/shard_map/all_gather | solution.py:70
  8.8 116.8 %reduce-scatter.7.cloned.1.call-start = ((), (), s32[]{:S(2)}) async-start(), calls=%async_computation.6 | async-start | bytes 294912 | tf_op jit(solution)/shard_map/reduce_scatter | solution.py:36
  89.8 3.0 copy-start.14
  89.8 35.8 %copy-start.7 = (bf16[4,1,1,128,128]{4,3,2,1,0:T(8,128)(2,1)S(1)}, bf16[4,1,1,128,128]{4,3,2,1,0:T(8,128)(2,1)}, u32[]{:S(2)}) copy-start(bf16[4,1,1,128,128]{4,3,2,1,0:T(8,128)(2,1)} %param.7) | copy-start | bytes 393220
  89.8 37.6 %copy-start.1 = (bf16[4096,128]{1,0:T(8,128)(2,1)S(1)}, bf16[4096,128]{1,0:T(8,128)(2,1)}, u32[]{:S(2)}) copy-start(bf16[4096,128]{1,0:T(8,128)(2,1)} %all-gather.10.cloned.1.call-done) | copy-start | bytes 3145732
  92.7 108.9 %all-gather.12.cloned.1.call-start = ((), (), s32[]{:S(2)}) async-start(), calls=%async_computation.13 | async-start | bytes 1081344 | tf_op jit(solution)/shard_map/all_gather | solution.py:70
  127.2 113.3 %reduce-scatter.9.cloned.1.call-start = ((), (), s32[]{:S(2)}) async-start(), calls=%async_computation.7 | async-start | bytes 294912 | tf_op jit(solution)/shard_map/reduce_scatter | solution.py:36
  204.6 37.8 %copy-start.2 = (bf16[4096,128]{1,0:T(8,128)(2,1)S(1)}, bf16[4096,128]{1,0:T(8,128)(2,1)}, u32[]{:S(2)}) copy-start(bf16[4096,128]{1,0:T(8,128)(2,1)} %all-gather.12.cloned.1.call-done) | copy-start | bytes 3145732
  207.5 108.4 %all-gather.14.cloned.1.call-start = ((), (), s32[]{:S(2)}) async-start(), calls=%async_computation.14 | async-start | bytes 1081344 | tf_op jit(solution)/shard_map/all_gather | solution.py:70
  242.0 118.4 %reduce-scatter.11.cloned.1.call-start = ((), (), s32[]{:S(2)}) async-start(), calls=%async_computation.8 | async-start | bytes 294912 | tf_op jit(solution)/shard_map/reduce_scatter | solution.py:36
  318.0 1.6 copy-start.3
  322.0 2.6 copy-start.6
  327.4 282.4 %reduce-scatter.13.cloned.1.call-start = ((), (), s32[]{:S(2)}) async-start(), calls=%async_computation.9 | async-start | bytes 1081344 | tf_op jit(solution)/shard_map/reduce_scatter | solution.py:95
  361.2 0.8 copy-start.12
  388.4 5.2 copy-start
  388.4 5.2 copy-start.18
  400.2 448.1 %reduce-scatter.15.cloned.1.call-start = ((), (), s32[]{:S(2)}) async-start(), calls=%async_computation.10 | async-start | bytes 1081344 | tf_op jit(solution)/shard_map/reduce_scatter | solution.py:95
  405.4 204.4 %copy-start.10 = (bf16[128,128]{0,1:T(8,128)(2,1)S(1)}, bf16[128,128]{0,1:T(8,128)(2,1)}, u32[]{:S(2)}) copy-start(bf16[128,128]{0,1:T(8,128)(2,1)} %convolution_convert_fusion.1) | copy-start | bytes 98308
  631.2 2.3 copy-start.17
  633.6 5.2 copy-start.5
  642.0 444.2 %reduce-scatter.17.cloned.1.call-start = ((), (), s32[]{:S(2)}) async-start(), calls=%async_computation.11 | async-start | bytes 1081344 | tf_op jit(solution)/shard_map/reduce_scatter | solution.py:95
  646.8 201.6 %copy-start.9 = (bf16[128,128]{0,1:T(8,128)(2,1)S(1)}, bf16[128,128]{0,1:T(8,128)(2,1)}, u32[]{:S(2)}) copy-start(bf16[128,128]{0,1:T(8,128)(2,1)} %convolution_convert_fusion.2) | copy-start | bytes 98308
  871.5 5.2 copy-start.4
  876.7 3.4 copy-start.8
  876.7 3.4 copy-start.11
  876.7 3.4 copy-start.13
  876.7 210.5 %copy-start.15 = (f32[128,128]{1,0:T(8,128)S(1)}, f32[128,128]{1,0:T(8,128)}, u32[]{:S(2)}) copy-start(f32[128,128]{1,0:T(8,128)} %get-tuple-element.31) | copy-start | bytes 196612
  876.7 210.5 %copy-start.16 = (f32[128,128]{1,0:T(8,128)S(1)}, f32[128,128]{1,0:T(8,128)}, u32[]{:S(2)}) copy-start(f32[128,128]{1,0:T(8,128)} %get-tuple-element.29) | copy-start | bytes 196612
Sparse Core Ops, SparseCore 0:
  11.2 75.6 all-gather.9
  92.8 32.7 reduce-scatter.6
  128.6 72.9 all-gather.11
  207.6 32.7 reduce-scatter.8
  242.9 72.9 all-gather.13
  327.5 32.7 reduce-scatter.10
  400.3 209.4 reduce-scatter.12
  642.2 206.1 reduce-scatter.14
  880.1 206.0 reduce-scatter.16
where the time goes:
time: 1110 us; the launch traced here: 1090 us
  waiting for transfers between devices  910 us (82%)
  matrix products  71.6 us (6%)
  blocking collectives  50.4 us (5%)
  local copies, waits for them, and re-layouts  36.9 us (3%)
  between operations  14.5 us (1%)
    reduce_scatter x3, waiting for transfers between devices, body(): lax.psum_scatter((near_part + far_part).astype(jnp.bfloat16), 'col', scat...  599 us
    all_gather x3, waiting for transfers between devices, body(): gathered = lax.all_gather(solved[None], 'col', axis=0, tiled=True)  214 us
    reduce_scatter x3, waiting for transfers between devices, reduce_rows(): lax.psum_scatter(pending_sum.astype(jnp.bfloat16), 'row', scatter_dimensi...  97.1 us
    all_gather x3, blocking collectives, gather_column(): lax.all_gather(back_value.astype(jnp.bfloat16)[None], 'row', axis=0, tile...  50.4 us
    dot_general x6, matrix products, backward_terms(): jnp.dot(onehot, flattened, precision=lax.Precision.HIGHEST, preferred_ele...  31.3 us
  transfers between devices with their start and end apart: 9, of which 9 were waited for; matrix products, arithmetic and copies ran while one was open for 3% of the time, Pallas kernels for 0%

commit v1 on v0

v1 whole, which is shorter than its diff:
```python
import jax
import jax.numpy as jnp
from jax import lax
from jax.experimental import pallas as pl
from jax.experimental.pallas import tpu as pltpu
from jax.sharding import PartitionSpec as P

CHAINS = 2
MESH = pl.DeviceIdType.MESH
BF16 = jnp.bfloat16
F32 = jnp.float32
LEVELS = 4
LOWER = 3
ROWS = 8
COLS = 32
DEEP = 8
WIDE = 4
PER = 6
HALF = ROWS * PER
N = 128


def dot_nt(a, b):
    return lax.dot_general(a, b, (((1,), (1,)), ((), ())), preferred_element_type=F32)


def dot_nn(a, b):
    return jnp.dot(a, b, preferred_element_type=F32)


def kernel(span, slots, order, target, keep, last, has, rs_hbm, inv_hbm, blk_hbm, sol_out, back_out, *scratch):
    it = iter(scratch)
    chains = N // span
    rs, inv, rs_t, sol_t, back_t = [next(it) for _ in range(5)]
    blk = [next(it) for _ in range(LOWER)]

    def per_pair():
        return [[next(it) for _ in range(chains)] for _ in range(LOWER)]

    gathered, part_out, part_in, copies = per_pair(), per_pair(), per_pair(), per_pair()
    seg, ry, rz, s2, s3, fz, fy = [per_pair() for _ in range(7)]
    pending = [[next(it) for _ in range(chains)] for _ in range(2)]
    own_part, far_scan, near_scan = [[next(it) for _ in range(chains)] for _ in range(3)]
    in_sem, z_sem, f_sem, b_sem = [next(it) for _ in range(4)]

    r = lax.axis_index("row")
    c = lax.axis_index("col")
    z = lax.div(c, WIDE)
    y = lax.rem(c, WIDE)

    def z_peer(d):
        return (r, lax.rem(z + d, DEEP) * WIDE + y)

    def y_peer(d):
        return (r, z * WIDE + lax.rem(y + d, WIDE))

    def row_peer(d):
        return (lax.rem(r + d, ROWS), c)

    def send(src, dst, send_sem, recv_sem, device):
        pltpu.make_async_remote_copy(
            src_ref=src, dst_ref=dst, send_sem=send_sem, recv_sem=recv_sem,
            device_id=device, device_id_type=MESH,
        ).start()

    def wait_for(ref, sem):
        pltpu.make_async_copy(ref, ref, sem).wait()

    barrier = pltpu.get_barrier_semaphore()
    for d in range(1, DEEP):
        pl.semaphore_signal(barrier, inc=1, device_id=z_peer(d), device_id_type=MESH)
    for d in range(1, ROWS):
        pl.semaphore_signal(barrier, inc=1, device_id=row_peer(d), device_id_type=MESH)
    for d in range(1, WIDE):
        pl.semaphore_signal(barrier, inc=1, device_id=y_peer(d), device_id_type=MESH)

    loads = [
        pltpu.make_async_copy(rs_hbm, rs, in_sem.at[0]),
        pltpu.make_async_copy(inv_hbm, inv, in_sem.at[1]),
    ] + [pltpu.make_async_copy(blk_hbm.at[l], blk[l], in_sem.at[2 + l]) for l in range(LOWER)]
    for load in loads:
        load.start()
    loads[0].wait()
    for l in range(LEVELS):
        rs_t[l] = rs[l].T
    loads[1].wait()

    def part(ch):
        return pl.ds(ch * span, span)

    def solve(level, ch, rhs):
        solved = dot_nt(rhs.astype(BF16), inv[level]).astype(BF16)
        sol_t[level, part(ch)] = solved.astype(F32)
        return solved

    def spread_column(l, ch):
        buf = gathered[l][ch]
        k = l * chains + ch
        own = buf.at[y]
        for d in (2, 1, 3):
            send(own, buf.at[y], f_sem.at[k, 0], f_sem.at[k, 1], y_peer(d))
        for d in (4, 3, 5, 2, 6):
            send(own, buf.at[(DEEP - d) * WIDE + y], f_sem.at[k, 0], z_sem.at[k, DEEP - d - 2], z_peer(d))

    def relay_column(l, ch):
        buf = gathered[l][ch]
        k = l * chains + ch
        wait_for(buf.at[pl.ds(0, 3)], f_sem.at[k, 1])
        here = buf.at[pl.ds(0, WIDE)]
        send(here, buf.at[pl.ds(7 * WIDE, WIDE)], f_sem.at[k, 0], f_sem.at[k, 2], z_peer(1))
        send(here, buf.at[pl.ds(WIDE, WIDE)], f_sem.at[k, 0], f_sem.at[k, 2], z_peer(7))
        for zr in (2, 6, 3, 5, 4):
            wait_for(buf.at[pl.ds(0, 1)], z_sem.at[k, zr - 2])
            got = buf.at[zr * WIDE + y]
            for d in (2, 1, 3):
                send(got, got, f_sem.at[k, 0], f_sem.at[k, 2], y_peer(d))

    def forward_term(l, h, ch, t):
        base = (l * 2 + h) * HALF + t * PER
        buf = gathered[l][ch]
        xs = jnp.concatenate([buf[slots[base + i]] for i in range(PER)], axis=1)
        ws = jnp.concatenate([blk[l][h * HALF + t * PER + i] for i in range(PER)], axis=1)
        return dot_nt(xs, ws)

    def near_forward(l, ch):
        k = l * chains + ch
        wait_for(gathered[l][ch].at[pl.ds(0, 23)], f_sem.at[k, 2])

        def total(t):
            value = forward_term(l, 0, ch, t)
            if l == 2:
                value = value + forward_term(l, 1, ch, t)
            if l > 0:
                value = value + pending[l - 1][ch][t]
            return value

        def step(i, carry):
            d = 1 + lax.rem(i + 2, 7)
            t = lax.rem(r + d, ROWS)
            part_out[l][ch][t] = total(t).astype(BF16)
            send(part_out[l][ch].at[t], part_in[l][ch].at[d - 1], f_sem.at[k, 3], f_sem.at[k, 4], row_peer(d))
            return carry

        lax.fori_loop(0, 7, step, 0, unroll=True)
        own_part[ch][...] = total(r)

    def far_forward(l, ch):
        def step(t, carry):
            pending[l][ch][t] = forward_term(l, 1, ch, t)
            return carry

        lax.fori_loop(0, ROWS, step, 0, unroll=2)

    def spread_row(level, ch, value):
        buf = copies[level - 1][ch]
        k = (level - 1) * chains + ch
        buf[r] = value
        for d in (4, 5, 3, 2, 6, 7, 1):
            send(buf.at[r], buf.at[r], b_sem.at[k, 0], b_sem.at[k, 1], row_peer(d))

    def next_forward(level, ch):
        l = level - 1
        k = l * chains + ch
        wait_for(part_in[l][ch], f_sem.at[k, 4])
        update = own_part[ch][...]
        for i in range(7):
            update = update + part_in[l][ch][i].astype(F32)
        solved = solve(level, ch, rs_t[level, part(ch)] - update)
        if level < LOWER:
            gathered[level][ch][y] = solved
            spread_column(level, ch)
        else:
            back = dot_nn(solved, inv[level])
            back_t[level, part(ch)] = back
            spread_row(level, ch, back.astype(BF16))

    def scan(l, h, ch, buf, out):
        base = (l * 2 + h) * HALF

        def step(i, total):
            term = dot_nn(buf[target[base + i]], blk[l][order[base + i]])
            total = total * keep[base + i] + term
            out[i] = total
            return total

        lax.fori_loop(0, HALF, step, jnp.zeros((span, N), F32), unroll=8)

    def near_backward(l, ch):
        k = l * chains + ch
        level = l + 1
        buf = copies[l][ch]
        wait_for(buf.at[pl.ds(0, 7)], b_sem.at[k, 1])
        scan(l, 0, ch, buf, near_scan[ch])
        if l == 2:
            scan(l, 1, ch, buf, far_scan[ch])
        near, far = l * 2 * COLS, (l * 2 + 1) * COLS

        def step(i, carry):
            for w in range(WIDE):
                j = i * WIDE + w
                value = near_scan[ch][last[near + j]] * has[near + j]
                value = value + far_scan[ch][last[far + j]] * has[far + j]
                seg[l][ch][i, w] = value.astype(BF16)
            return carry

        lax.fori_loop(0, DEEP, step, 0, unroll=2)
        for d in (2, 1, 3):
            send(seg[l][ch].at[pl.ds(2, 5), lax.rem(y + d, WIDE)], ry[l][ch].at[d - 1],
                 b_sem.at[k, 2], b_sem.at[k, 3], y_peer(d))
        send(seg[l][ch].at[1], rz[l][ch].at[0], b_sem.at[k, 2], b_sem.at[k, 4], z_peer(1))
        send(seg[l][ch].at[7], rz[l][ch].at[1], b_sem.at[k, 2], b_sem.at[k, 4], z_peer(7))

    def far_backward(l, ch):
        scan(l, 1, ch, copies[l + 1][ch], far_scan[ch])

    def relay_backward(l, ch):
        k = l * chains + ch
        wait_for(ry[l][ch], b_sem.at[k, 3])
        for i in (2, 1, 3, 0, 4):
            value = seg[l][ch][i + 2, y].astype(F32)
            for d in range(3):
                value = value + ry[l][ch][d, i].astype(F32)
            s2[l][ch][i] = value.astype(BF16)
            send(s2[l][ch].at[i], fz[l][ch].at[i], b_sem.at[k, 2], b_sem.at[k, 5], z_peer(i + 2))
        wait_for(rz[l][ch], b_sem.at[k, 4])
        for d in (2, 1, 3):
            other = lax.rem(y + d, WIDE)
            value = seg[l][ch][0, other].astype(F32)
            for e in range(2):
                value = value + rz[l][ch][e, other].astype(F32)
            s3[l][ch][d - 1] = value.astype(BF16)
            send(s3[l][ch].at[d - 1], fy[l][ch].at[d - 1], b_sem.at[k, 2], b_sem.at[k, 6], y_peer(d))

    def next_backward(l, ch):
        k = l * chains + ch
        update = seg[l][ch][0, y].astype(F32)
        for e in range(2):
            update = update + rz[l][ch][e, y].astype(F32)
        wait_for(fy[l][ch], b_sem.at[k, 6])
        for i in range(3):
            update = update + fy[l][ch][i].astype(F32)
        wait_for(fz[l][ch], b_sem.at[k, 5])
        for i in range(5):
            update = update + fz[l][ch][i].astype(F32)
        rhs = (sol_t[l, part(ch)] - update).astype(BF16)
        back = dot_nn(rhs, inv[l])
        back_t[l, part(ch)] = back
        if l > 0:
            spread_row(l, ch, back.astype(BF16))

    def finish(level):
        back_out[level] = back_t[level].T

    for ch in range(chains):
        gathered[0][ch][y] = solve(0, ch, rs_t[0, part(ch)])
    pl.semaphore_wait(barrier, 17)
    for ch in range(chains):
        spread_column(0, ch)
    for l in range(LOWER):
        for ch in range(chains):
            relay_column(l, ch)
        loads[2 + l].wait()
        for ch in range(chains):
            near_forward(l, ch)
        for ch in range(chains):
            if l < 2:
                far_forward(l, ch)
            next_forward(l + 1, ch)
    for l in (2, 1, 0):
        for ch in range(chains):
            near_backward(l, ch)
        if l == 2:
            for level in range(LEVELS):
                sol_out[level] = sol_t[level].T.astype(BF16)
        else:
            finish(l + 2)
        for ch in range(chains):
            if l > 0:
                far_backward(l - 1, ch)
            relay_backward(l, ch)
        for ch in range(chains):
            next_backward(l, ch)
    finish(1)
    finish(0)
    for l in range(LOWER):
        for ch in range(chains):
            k = l * chains + ch
            wait_for(gathered[l][ch].at[pl.ds(0, 31)], f_sem.at[k, 0])
            wait_for(part_in[l][ch], f_sem.at[k, 3])
            wait_for(copies[l][ch].at[pl.ds(0, 7)], b_sem.at[k, 0])
            wait_for(gathered[l][ch].at[pl.ds(0, 31)], b_sem.at[k, 2])


def index_tables(sources, z):
    src = sources.reshape(LOWER * 2, HALF)
    slots = lax.rem(lax.div(src, WIDE) + DEEP - z, DEEP) * WIDE + lax.rem(src, WIDE)
    place = jnp.arange(HALF, dtype=jnp.int32)
    a, b = src[:, :, None], src[:, None, :]
    before = (b < a) | ((b == a) & (place[None, None, :] < place[None, :, None]))
    rank = jnp.sum(before.astype(jnp.int32), axis=2)
    pick = rank[:, None, :] == place[None, :, None]
    order = jnp.sum(jnp.where(pick, place[None, None, :], 0), axis=2)
    ordered = jnp.sum(jnp.where(pick, src[:, None, :], 0), axis=2)
    previous = jnp.concatenate([jnp.full((LOWER * 2, 1), -1, jnp.int32), ordered[:, :-1]], axis=1)
    keep = (ordered == previous).astype(F32)
    slot = jnp.arange(COLS, dtype=jnp.int32)
    column = lax.rem(lax.div(slot, WIDE) + z, DEEP) * WIDE + lax.rem(slot, WIDE)
    upto = jnp.sum((src[:, None, :] <= column[None, :, None]).astype(jnp.int32), axis=2)
    has = jnp.any(src[:, None, :] == column[None, :, None], axis=2).astype(F32)
    last = jnp.maximum(upto - 1, 0)
    shift = jnp.arange(LOWER * 2, dtype=jnp.int32)[:, None] % 2 * HALF
    return (slots.reshape(-1), (order + shift).reshape(-1), (order // PER).reshape(-1),
            keep.reshape(-1), last.reshape(-1), has.reshape(-1))


def body(right_sides, inverses, blocks, sources):
    chains = CHAINS
    span = N // chains
    z = lax.div(lax.axis_index("col"), WIDE)
    tables = index_tables(sources, z)

    def tile(*lead, dtype=BF16):
        return pltpu.VMEM((*lead, span, N), dtype)

    def per_pair(*lead):
        return [tile(*lead) for _ in range(LOWER * chains)]

    scratch = [
        pltpu.VMEM((LEVELS, N, N), F32),
        pltpu.VMEM((LEVELS, N, N), BF16),
        pltpu.VMEM((LEVELS, N, N), F32),
        pltpu.VMEM((LEVELS, N, N), F32),
        pltpu.VMEM((LEVELS, N, N), F32),
    ]
    scratch += [pltpu.VMEM((2 * HALF, N, N), BF16) for _ in range(LOWER)]
    scratch += per_pair(COLS) + per_pair(ROWS) + per_pair(ROWS - 1) + per_pair(ROWS)
    scratch += per_pair(DEEP, WIDE) + per_pair(3, 5) + per_pair(2, WIDE) + per_pair(5) + per_pair(3)
    scratch += per_pair(5) + per_pair(3)
    scratch += [tile(ROWS, dtype=F32) for _ in range(2 * chains)]
    scratch += [tile(dtype=F32) for _ in range(chains)]
    scratch += [tile(HALF, dtype=F32) for _ in range(2 * chains)]
    scratch += [
        pltpu.SemaphoreType.DMA((2 + LOWER,)),
        pltpu.SemaphoreType.DMA((LOWER * chains, 5)),
        pltpu.SemaphoreType.DMA((LOWER * chains, 5)),
        pltpu.SemaphoreType.DMA((LOWER * chains, 7)),
    ]
    smem = pl.BlockSpec(memory_space=pltpu.SMEM)
    vmem = pl.BlockSpec(memory_space=pltpu.VMEM)
    hbm = pl.BlockSpec(memory_space=pl.ANY)

    def run(*refs):
        kernel(span, *refs)

    solved, back = pl.pallas_call(
        run,
        out_shape=(
            jax.ShapeDtypeStruct((LEVELS, N, N), BF16),
            jax.ShapeDtypeStruct((LEVELS, N, N), F32),
        ),
        in_specs=[smem] * 6 + [hbm] * 3,
        out_specs=(vmem, vmem),
        scratch_shapes=scratch,
        compiler_params=pltpu.CompilerParams(
            collective_id=0, has_side_effects=True, vmem_limit_bytes=48 * 1024 * 1024
        ),
    )(*tables, right_sides[:, 0, 0], inverses[:, 0, 0],
      blocks[:, 0, 0].reshape(LOWER, 2 * HALF, N, N))
    return solved[:, None, None], back[:, None, None]


def solution(mesh):
    return jax.shard_map(
        body,
        mesh=mesh,
        in_specs=(
            P(None, "row", "col", None, None),
            P(None, "row", "col", None, None),
            P(None, "row", "col", None, None, None, None, None),
            P(None, "row", "col", None, None, None),
        ),
        out_specs=(P(None, "row", "col", None, None), P(None, "row", "col", None, None)),
        check_vma=False,
    )
```

time: 1110 us -> 124 us (0.11); the launches traced: 1090 us -> 124 us
  waiting for transfers between devices: 910 us -> 0 us
  Pallas kernels: 0 us -> 117 us
  matrix products: 71.6 us -> 0 us
  blocking collectives: 50.4 us -> 0 us
  local copies, waits for them, and re-layouts: 36.9 us -> 4.72 us
  between operations: 14.5 us -> 0.7 us
    reduce_scatter x6 -> x0, waiting for transfers between devices: 696 us -> none  [the longest x3 599 us: body(): lax.psum_scatter((near_part + far_part).astype(jnp.bfloat16), 'col', scat...]
    all_gather x3 -> x0, waiting for transfers between devices: 214 us -> none  [body(): gathered = lax.all_gather(solved[None], 'col', axis=0, tiled=True)]
    pallas_call x0 -> x1, Pallas kernels: none -> 117 us  [body(): pl.pallas_call(run, out_shape=(jax.ShapeDtypeStruct((LEVELS, N, N), BF16)...]
    dot_general x26 -> x0, matrix products: 71.6 us -> none  [the longest x6 31.3 us: backward_terms(): jnp.dot(onehot, flattened, precision=lax.Precision.HIGHEST, preferred_ele...]
    all_gather x3 -> x0, blocking collectives: 50.4 us -> none  [gather_column(): lax.all_gather(back_value.astype(jnp.bfloat16)[None], 'row', axis=0, tile...]
    gather x12 -> x0, local copies, waits for them, and re-layouts: 17 us -> none  [forward_terms(): chosen = jnp.take(gathered, sources[column_level, jump_index], axis=0)]
    dot_general x6 -> x0, local copies, waits for them, and re-layouts: 15.2 us -> none  [backward_terms(): jnp.einsum('tkab,tas->tkbs', blocks[column_level, jump_index], column_cop...]
  transfers between devices with their start and end apart: 9 -> 0, of which waited for: 9 -> 0; matrix products, arithmetic and copies ran while one was open for 3% -> 0% of each run, Pallas kernels for 0% -> 0%
where the time goes in v1:
time: 124 us
  Pallas kernels  117 us (94%)
  local copies, waits for them, and re-layouts  4.72 us (4%)
  other arithmetic  1.26 us (1%)
    pallas_call x1, Pallas kernels, body(): pl.pallas_call(run, out_shape=(jax.ShapeDtypeStruct((LEVELS, N, N), BF16)...  117 us
    unnamed x7, local copies, waits for them, and re-layouts  4.05 us

profile of v1, /device:TPU:1, one launch (start us, length us, event | category | flops | bytes accessed | tf_op | source)
XLA Modules:
  0.0 123.8 jit_solution(13544185108133959321)
XLA Ops:
  0.7 0.8 copy.12
  1.5 0.1 reshape.94
  1.6 0.1 lt.39
  1.7 0.3 convert_reduce_fusion
  2.0 0.2 compare_reduce_fusion
  2.3 0.1 reshape.101.refs_5_
  2.3 0.2 convert_reduce_fusion.1
  2.6 0.1 max.12.refs_4_
  2.7 0.3 select_reduce_fusion
  3.0 0.1 fusion
  3.0 0.1 and.48
  3.1 0.1 reshape.100.refs_3_
  3.2 0.1 broadcast_divide_fusion
  3.3 0.1 div.57
  3.4 0.1 add.60.refs_1_
  3.4 0.0 copy-start
  3.4 1.0 copy-done
  4.4 0.0 copy-start.1
  4.4 0.9 copy-done.1
  5.3 117.1 %shard_map.59 = (bf16[4,128,128]{2,1,0:T(8,128)(2,1)S(1)}, f32[4,128,128]{2,1,0:T(8,128)S(1)}) custom-call(s32[288]{0:T(512)S(1)} %fusion.5.refs_0_, s32[288]{0:T(512)S(1)} %add.60.refs_1_, s32[288]{0:T(512)S(1)} %add_select_fusion.refs_2_, f32[288]{0:T(512)S(1)} %reshape.100.refs_3_, s32[192]{0:T(256)S(1)} %max.12.refs_4_, f32[192]{0:T(256)S(1)} %reshape.101.refs_5_, ...), custom_call_target="tpu_custom_call" | custom-call | tf_op jit(solution)/shard_map/pallas_call | solution.py:355
  122.4 0.7 copy.18
  123.1 0.7 copy.19
  (7 shorter events, 0.1 us)
Async XLA Ops:
  3.4 1.0 copy-start
  4.4 0.9 copy-start.1

commit v2 on v1

v2 whole, which is shorter than its diff:
```python
import functools

import jax
import jax.numpy as jnp
from jax import lax
from jax.experimental import pallas as pl
from jax.experimental.pallas import tpu as pltpu
from jax.sharding import PartitionSpec as P

CHAINS = 4
MESH = pl.DeviceIdType.MESH
BF16 = jnp.bfloat16
F32 = jnp.float32
LEVELS = 4
LOWER = 3
ROWS = 8
COLS = 32
DEEP = 8
WIDE = 4
PER = 6
HALF = ROWS * PER
N = 128


def dot_nt(a, b):
    return lax.dot_general(a, b, (((1,), (1,)), ((), ())), preferred_element_type=F32)


def dot_nn(a, b):
    return jnp.dot(a, b, preferred_element_type=F32)


def index_tables(src, z, int_table, float_table):
    lane8 = lax.broadcasted_iota(jnp.int32, (8, N), 1)
    row8 = lax.broadcasted_iota(jnp.int32, (8, N), 0)

    def place(t, wide):
        for i in range(PER):
            here = lane8 == t * PER + i
            for lh in range(LOWER * 2):
                wide = jnp.where(here & (row8 == lh), src[lh // 2, i, lh % 2, t], wide)
        return wide

    wide = lax.fori_loop(0, ROWS, place, jnp.zeros((8, N), jnp.int32))
    tall = jnp.concatenate([wide, jnp.zeros((N - 8, N), jnp.int32)], axis=0).T
    first = lax.broadcasted_iota(jnp.int32, (HALF, N), 0)
    second = lax.broadcasted_iota(jnp.int32, (HALF, N), 1)
    lane = lax.broadcasted_iota(jnp.int32, (1, N), 1)
    column = (((lane >> 2) + z) & (DEEP - 1)) * WIDE + (lane & (WIDE - 1))
    group = lax.div(first, PER)

    def down(mask, value):
        return jnp.sum(jnp.where(mask, value, 0), axis=0, keepdims=True)

    def inside(value, limit):
        return jnp.minimum(jnp.maximum(value, 0), limit)

    for lh in range(LOWER * 2):
        a = jnp.broadcast_to(tall[0:HALF, lh:lh + 1], (HALF, N))
        b = jnp.broadcast_to(wide[lh:lh + 1, :], (HALF, N))
        before = ((b < a) | ((b == a) & (second < first))) & (second < HALF)
        rank = jnp.sum(jnp.where(before, 1, 0), axis=1, keepdims=True)
        pick = jnp.broadcast_to(rank, (HALF, N)) == second
        ordered = down(pick, a)
        same = (ordered == pltpu.roll(ordered, 1, 1)) & (lane > 0)
        int_table[0, lh:lh + 1, :] = inside(down(pick, first), HALF - 1) + (lh % 2) * HALF
        int_table[1, lh:lh + 1, :] = inside(down(pick, group), ROWS - 1)
        int_table[2, lh:lh + 1, :] = inside(down(a <= column, 1) - 1, HALF - 1)
        float_table[0, lh:lh + 1, :] = jnp.where(same, 1.0, 0.0)
        float_table[1, lh:lh + 1, :] = jnp.where(down(a == column, 1) > 0, 1.0, 0.0)


def kernel(span, src, rs_hbm, inv_hbm, blk_hbm, sol_out, back_out,
           rs, inv, rs_t, sol_t, back_t, blk, gathered, part_out, part_in, copies, seg, ry, rz, s2, s3,
           fz, fy, pending, held, held_back, near_scan, far_scan,
           int_vec, float_vec, ints, floats, in_sem, z_sem, f_sem, b_sem):
    chains = N // span
    r = lax.axis_index("row")
    c = lax.axis_index("col")
    z = lax.div(c, WIDE)
    y = lax.rem(c, WIDE)

    def z_peer(d):
        return (r, lax.rem(z + d, DEEP) * WIDE + y)

    def y_peer(d):
        return (r, z * WIDE + lax.rem(y + d, WIDE))

    def row_peer(d):
        return (lax.rem(r + d, ROWS), c)

    def send(src, dst, send_sem, recv_sem, device):
        pltpu.make_async_remote_copy(
            src_ref=src, dst_ref=dst, send_sem=send_sem, recv_sem=recv_sem,
            device_id=device, device_id_type=MESH,
        ).start()

    def wait_for(ref, sem):
        pltpu.make_async_copy(ref, ref, sem).wait()

    def each(count, step):
        def run(i, carry):
            step(i)
            return carry

        lax.fori_loop(0, count, run, 0)

    barrier = pltpu.get_barrier_semaphore()
    for d in range(1, DEEP):
        pl.semaphore_signal(barrier, inc=1, device_id=z_peer(d), device_id_type=MESH)
    for d in range(1, ROWS):
        pl.semaphore_signal(barrier, inc=1, device_id=row_peer(d), device_id_type=MESH)
    for d in range(1, WIDE):
        pl.semaphore_signal(barrier, inc=1, device_id=y_peer(d), device_id_type=MESH)

    load_rs = pltpu.make_async_copy(rs_hbm, rs, in_sem.at[0])
    load_inv = pltpu.make_async_copy(inv_hbm, inv, in_sem.at[1])

    def load_blk(l):
        return pltpu.make_async_copy(blk_hbm.at[l], blk.at[l], in_sem.at[2 + l])

    load_rs.start()
    load_inv.start()
    for l in range(LOWER):
        load_blk(l).start()
    pending[0] = jnp.zeros((ROWS, N, N), F32)
    load_rs.wait()

    rs_t[0] = rs[0].T
    load_inv.wait()

    def part(ch):
        return pl.ds(pl.multiple_of(ch * span, span), span)

    def solve(level, ch, rhs):
        solved = dot_nt(rhs.astype(BF16), inv[level]).astype(BF16)
        sol_t[level, part(ch)] = solved.astype(F32)
        return solved

    def spread_column(l, ch):
        buf = gathered.at[l, ch]
        k = l * chains + ch
        own = buf.at[y]
        for d in (2, 1, 3):
            send(own, buf.at[y], f_sem.at[k, 0], f_sem.at[k, 1], y_peer(d))
        for d in (4, 3, 5, 2, 6):
            send(own, buf.at[(DEEP - d) * WIDE + y], f_sem.at[k, 0], z_sem.at[k, DEEP - d - 2], z_peer(d))

    def relay_column(l, ch):
        buf = gathered.at[l, ch]
        k = l * chains + ch
        wait_for(buf.at[pl.ds(0, 3)], f_sem.at[k, 1])
        here = buf.at[pl.ds(0, WIDE)]
        send(here, buf.at[pl.ds(7 * WIDE, WIDE)], f_sem.at[k, 0], f_sem.at[k, 2], z_peer(1))
        send(here, buf.at[pl.ds(WIDE, WIDE)], f_sem.at[k, 0], f_sem.at[k, 2], z_peer(7))
        for zr in (2, 6, 3, 5, 4):
            wait_for(buf.at[pl.ds(0, 1)], z_sem.at[k, zr - 2])
            got = buf.at[zr * WIDE + y]
            for d in (2, 1, 3):
                send(got, got, f_sem.at[k, 0], f_sem.at[k, 2], y_peer(d))

    def forward_term(l, h, rows, t):
        def slot(i):
            column = src[l, i, h, t]
            return (((column >> 2) + (DEEP - z)) & (DEEP - 1)) * WIDE + (column & (WIDE - 1))

        xs = jnp.concatenate([held[slot(i), rows] for i in range(PER)], axis=1)
        ws = jnp.concatenate([blk[l, h * HALF + t * PER + i] for i in range(PER)], axis=1)
        return dot_nt(xs, ws)

    def near_forward(l, ch):
        k = l * chains + ch
        wait_for(gathered.at[l, ch, pl.ds(0, 23)], f_sem.at[k, 2])
        held[:, part(ch)] = gathered[l, ch]

        @pl.when(l == 2)
        def _():
            def step(t, carry):
                pending[2, t, part(ch)] = pending[2, t, part(ch)] + forward_term(l, 1, part(ch), t)
                return carry

            lax.fori_loop(0, ROWS, step, 0, unroll=True)

        def step(t, carry):
            value = forward_term(l, 0, part(ch), t) + pending[l, t, part(ch)]
            part_out[l, ch, t] = value.astype(BF16)
            return carry

        lax.fori_loop(0, ROWS, step, 0, unroll=True)
        for d in (4, 5, 3, 2, 6, 7, 1):
            t = lax.rem(r + d, ROWS)
            send(part_out.at[l, ch, t], part_in.at[l, ch, d - 1], f_sem.at[k, 3], f_sem.at[k, 4], row_peer(d))

    def far_forward(l):
        def step(t, carry):
            pending[lax.rem(l + 1, LOWER), t] = forward_term(l, 1, slice(None), t)
            return carry

        lax.fori_loop(0, ROWS, step, 0, unroll=True)

    def spread_row(level, ch, value):
        below = lax.rem(level + 2, LOWER)
        buf = copies.at[below, ch]
        k = below * chains + ch
        copies[below, ch, r] = value
        for d in (4, 5, 3, 2, 6, 7, 1):
            send(buf.at[r], buf.at[r], b_sem.at[k, 0], b_sem.at[k, 1], row_peer(d))

    def next_forward(l, ch):
        k = l * chains + ch
        level = l + 1
        wait_for(part_in.at[l, ch], f_sem.at[k, 4])
        update = part_out[l, ch, r].astype(F32)
        for i in range(7):
            update = update + part_in[l, ch, i].astype(F32)
        solved = solve(level, ch, rs_t[level, part(ch)] - update)

        @pl.when(level < LOWER)
        def _():
            gathered[lax.rem(level, LOWER), ch, y] = solved
            spread_column(lax.rem(level, LOWER), ch)

        @pl.when(level == LOWER)
        def _():
            back = dot_nn(solved, inv[LOWER])
            back_t[LOWER, part(ch)] = back
            spread_row(LOWER, ch, back.astype(BF16))

    def scan(l, h, out, rows, count):
        lh = l * 2 + h

        def step(i, total):
            value = held_back[ints[1, lh, i], rows]
            total = total * floats[0, lh, i] + dot_nn(value, blk[l, ints[0, lh, i]])
            out[i, rows] = total
            return total

        lax.fori_loop(0, HALF, step, jnp.zeros((count, N), F32), unroll=True)

    def near_backward(l, ch):
        k = l * chains + ch
        wait_for(copies.at[l, ch, pl.ds(0, 7)], b_sem.at[k, 1])
        held_back[:, part(ch)] = copies[l, ch]

        @pl.when(l == 2)
        def _():
            scan(l, 1, far_scan, part(ch), span)

        scan(l, 0, near_scan, part(ch), span)
        near, far = l * 2, l * 2 + 1

        def step(i, carry):
            for w in range(WIDE):
                j = i * WIDE + w
                value = near_scan[ints[2, near, j], part(ch)] * floats[1, near, j]
                value = value + far_scan[ints[2, far, j], part(ch)] * floats[1, far, j]
                seg[l, ch, i, w] = value.astype(BF16)
            return carry

        lax.fori_loop(0, DEEP, step, 0, unroll=2)
        for d in (2, 1, 3):
            send(seg.at[l, ch, pl.ds(2, 5), lax.rem(y + d, WIDE)], ry.at[l, ch, d - 1],
                 b_sem.at[k, 2], b_sem.at[k, 3], y_peer(d))
        send(seg.at[l, ch, 1], rz.at[l, ch, 0], b_sem.at[k, 2], b_sem.at[k, 4], z_peer(1))
        send(seg.at[l, ch, 7], rz.at[l, ch, 1], b_sem.at[k, 2], b_sem.at[k, 4], z_peer(7))

    def relay_backward(l, ch):
        k = l * chains + ch
        wait_for(ry.at[l, ch], b_sem.at[k, 3])
        for i in (2, 1, 3, 0, 4):
            value = seg[l, ch, i + 2, y].astype(F32)
            for d in range(3):
                value = value + ry[l, ch, d, i].astype(F32)
            s2[l, ch, i] = value.astype(BF16)
            send(s2.at[l, ch, i], fz.at[l, ch, i], b_sem.at[k, 2], b_sem.at[k, 5], z_peer(i + 2))
        wait_for(rz.at[l, ch], b_sem.at[k, 4])
        for d in (2, 1, 3):
            other = lax.rem(y + d, WIDE)
            value = seg[l, ch, 0, other].astype(F32)
            for e in range(2):
                value = value + rz[l, ch, e, other].astype(F32)
            s3[l, ch, d - 1] = value.astype(BF16)
            send(s3.at[l, ch, d - 1], fy.at[l, ch, d - 1], b_sem.at[k, 2], b_sem.at[k, 6], y_peer(d))

    def next_backward(l, ch):
        k = l * chains + ch
        update = seg[l, ch, 0, y].astype(F32)
        for e in range(2):
            update = update + rz[l, ch, e, y].astype(F32)
        wait_for(fy.at[l, ch], b_sem.at[k, 6])
        for i in range(3):
            update = update + fy[l, ch, i].astype(F32)
        wait_for(fz.at[l, ch], b_sem.at[k, 5])
        for i in range(5):
            update = update + fz[l, ch, i].astype(F32)
        rhs = (sol_t[l, part(ch)] - update).astype(BF16)
        back = dot_nn(rhs, inv[l])
        back_t[l, part(ch)] = back

        @pl.when(l > 0)
        def _():
            spread_row(l, ch, back.astype(BF16))

    @functools.partial(each, chains)
    def _(ch):
        gathered[0, ch, y] = solve(0, ch, rs_t[0, part(ch)])

    pl.semaphore_wait(barrier, 17)
    each(chains, lambda ch: spread_column(0, ch))
    index_tables(src, z, int_vec, float_vec)
    move_ints = pltpu.make_async_copy(int_vec, ints, in_sem.at[2 + LOWER])
    move_floats = pltpu.make_async_copy(float_vec, floats, in_sem.at[3 + LOWER])
    move_ints.start()
    move_floats.start()

    @functools.partial(each, LOWER)
    def _(i):
        rs_t[i + 1] = rs[i + 1].T

    move_ints.wait()
    move_floats.wait()

    @functools.partial(each, LOWER)
    def _(l):
        each(chains, lambda ch: relay_column(l, ch))
        load_blk(l).wait()
        each(chains, lambda ch: near_forward(l, ch))

        @pl.when(l < 2)
        def _():
            far_forward(l)

        each(chains, lambda ch: next_forward(l, ch))

    @functools.partial(each, LOWER)
    def _(step):
        l = 2 - step
        each(chains, lambda ch: near_backward(l, ch))

        @pl.when(l > 0)
        def _():
            scan(lax.rem(l + 2, LOWER), 1, far_scan, slice(None), N)

        sol_out[l + 1] = sol_t[l + 1].T.astype(BF16)
        back_out[l + 1] = back_t[l + 1].T
        each(chains, lambda ch: relay_backward(l, ch))
        each(chains, lambda ch: next_backward(l, ch))

    sol_out[0] = sol_t[0].T.astype(BF16)
    back_out[0] = back_t[0].T

    @functools.partial(each, LOWER * chains)
    def _(k):
        l, ch = lax.div(k, chains), lax.rem(k, chains)
        wait_for(gathered.at[l, ch, pl.ds(0, 31)], f_sem.at[k, 0])
        wait_for(part_in.at[l, ch], f_sem.at[k, 3])
        wait_for(copies.at[l, ch, pl.ds(0, 7)], b_sem.at[k, 0])
        wait_for(gathered.at[l, ch, pl.ds(0, 31)], b_sem.at[k, 2])


def body(right_sides, inverses, blocks, sources):
    chains = CHAINS
    span = N // chains

    def tile(*lead):
        return pltpu.VMEM((LOWER, chains, *lead, span, N), BF16)

    def whole(*lead, dtype=F32):
        return pltpu.VMEM((*lead, N, N), dtype)

    scratch = [
        whole(LEVELS), whole(LEVELS, dtype=BF16), whole(LEVELS), whole(LEVELS), whole(LEVELS),
        whole(LOWER, 2 * HALF, dtype=BF16),
        tile(COLS), tile(ROWS), tile(ROWS - 1), tile(ROWS),
        tile(DEEP, WIDE), tile(3, 5), tile(2, WIDE), tile(5), tile(3), tile(5), tile(3),
        whole(LOWER, ROWS), whole(COLS, dtype=BF16), whole(ROWS, dtype=BF16), whole(HALF), whole(HALF),
        pltpu.VMEM((3, 8, N), jnp.int32), pltpu.VMEM((2, 8, N), F32),
        pltpu.SMEM((3, 8, N), jnp.int32), pltpu.SMEM((2, 8, N), F32),
        pltpu.SemaphoreType.DMA((4 + LOWER,)),
        pltpu.SemaphoreType.DMA((LOWER * chains, 5)),
        pltpu.SemaphoreType.DMA((LOWER * chains, 5)),
        pltpu.SemaphoreType.DMA((LOWER * chains, 7)),
    ]
    smem = pl.BlockSpec(memory_space=pltpu.SMEM)
    vmem = pl.BlockSpec(memory_space=pltpu.VMEM)
    hbm = pl.BlockSpec(memory_space=pl.ANY)

    def run(*refs):
        kernel(span, *refs)

    solved, back = pl.pallas_call(
        run,
        out_shape=(
            jax.ShapeDtypeStruct((LEVELS, N, N), BF16),
            jax.ShapeDtypeStruct((LEVELS, N, N), F32),
        ),
        in_specs=[smem] + [hbm] * 3,
        out_specs=(vmem, vmem),
        scratch_shapes=scratch,
        compiler_params=pltpu.CompilerParams(
            collective_id=0, has_side_effects=True, vmem_limit_bytes=60 * 1024 * 1024
        ),
    )(jnp.transpose(sources[:, 0, 0], (0, 3, 1, 2)), right_sides[:, 0, 0], inverses[:, 0, 0],
      blocks[:, 0, 0].reshape(LOWER, 2 * HALF, N, N))
    return solved[:, None, None], back[:, None, None]


def solution(mesh):
    return jax.shard_map(
        body,
        mesh=mesh,
        in_specs=(
            P(None, "row", "col", None, None),
            P(None, "row", "col", None, None),
            P(None, "row", "col", None, None, None, None, None),
            P(None, "row", "col", None, None, None),
        ),
        out_specs=(P(None, "row", "col", None, None), P(None, "row", "col", None, None)),
        check_vma=False,
    )
```

time: 124 us -> 111 us (0.90)
  Pallas kernels: 117 us -> 107 us
  local copies, waits for them, and re-layouts: 4.72 us -> 3.24 us
  other arithmetic: 1.26 us -> 0 us
    pallas_call x1, Pallas kernels: 117 us -> 107 us  [body(): pl.pallas_call(run, out_shape=(jax.ShapeDtypeStruct((LEVELS, N, N), BF16)...]
    unnamed x7 -> x2, local copies, waits for them, and re-layouts: 4.05 us -> 3.24 us
where the time goes in v2:
time: 111 us
  Pallas kernels  107 us (96%)
  local copies, waits for them, and re-layouts  3.24 us (3%)
    pallas_call x1, Pallas kernels, body(): pl.pallas_call(run, out_shape=(jax.ShapeDtypeStruct((LEVELS, N, N), BF16)...  107 us
    unnamed x2, local copies, waits for them, and re-layouts  3.24 us

profile of v2, /device:TPU:1, one launch (start us, length us, event | category | flops | bytes accessed | tf_op | source)
XLA Modules:
  0.0 111.0 jit_solution(6664859093835207653)
XLA Ops:
  0.6 107.1 %shard_map.59 = (bf16[4,128,128]{2,1,0:T(8,128)(2,1)}, f32[4,128,128]{2,1,0:T(8,128)}) custom-call(s32[3,6,2,8]{3,2,1,0:T(2,128)} %bitcast.17, f32[4,128,128]{2,1,0:T(8,128)} %bitcast.13, bf16[4,128,128]{2,1,0:T(8,128)(2,1)} %bitcast.15, bf16[3,96,128,128]{3,2,1,0:T(8,128)(2,1)} %bitcast.12), custom_call_target="tpu_custom_call" | custom-call | tf_op jit(solution)/shard_map/pallas_call | solution.py:391
  107.8 1.6 %copy.10 = bf16[4,1,1,128,128]{4,3,2,1,0:T(8,128)(2,1)} copy(bf16[4,1,1,128,128]{4,3,2,1,0:T(8,128)(2,1)} %bitcast.16) | data formatting | bytes 262144
  109.3 1.7 %copy.11 = f32[4,1,1,128,128]{4,3,2,1,0:T(8,128)} copy(f32[4,1,1,128,128]{4,3,2,1,0:T(8,128)} %bitcast.14) | data formatting | bytes 524288

commit v3 on v2

--- a/solution.py
+++ b/solution.py
@@ -98,12 +98,23 @@
     def wait_for(ref, sem):
         pltpu.make_async_copy(ref, ref, sem).wait()
 
-    def each(count, step):
+    def each(count, step, start=0):
         def run(i, carry):
             step(i)
             return carry
 
-        lax.fori_loop(0, count, run, 0)
+        lax.fori_loop(start, count, run, 0)
+
+    half = chains // 2
+
+    def early(step):
+        each(half, step)
+
+    def late(step):
+        each(chains, step, half)
+
+    early_rows = pl.ds(0, half * span)
+    late_rows = pl.ds(half * span, half * span)
 
     barrier = pltpu.get_barrier_semaphore()
     for d in range(1, DEEP):
@@ -191,12 +202,14 @@
             t = lax.rem(r + d, ROWS)
             send(part_out.at[l, ch, t], part_in.at[l, ch, d - 1], f_sem.at[k, 3], f_sem.at[k, 4], row_peer(d))
 
-    def far_forward(l):
-        def step(t, carry):
-            pending[lax.rem(l + 1, LOWER), t] = forward_term(l, 1, slice(None), t)
-            return carry
-
-        lax.fori_loop(0, ROWS, step, 0, unroll=True)
+    def far_forward(l, rows):
+        @pl.when(l < 2)
+        def _():
+            def step(t, carry):
+                pending[lax.rem(l + 1, LOWER), t, rows] = forward_term(l, 1, rows, t)
+                return carry
+
+            lax.fori_loop(0, ROWS, step, 0, unroll=True)
 
     def spread_row(level, ch, value):
         below = lax.rem(level + 2, LOWER)
@@ -306,7 +319,7 @@
         gathered[0, ch, y] = solve(0, ch, rs_t[0, part(ch)])
 
     pl.semaphore_wait(barrier, 17)
-    each(chains, lambda ch: spread_column(0, ch))
+    early(lambda ch: spread_column(0, ch))
     index_tables(src, z, int_vec, float_vec)
     move_ints = pltpu.make_async_copy(int_vec, ints, in_sem.at[2 + LOWER])
     move_floats = pltpu.make_async_copy(float_vec, floats, in_sem.at[3 + LOWER])
@@ -320,32 +333,54 @@
     move_ints.wait()
     move_floats.wait()
 
+    def far_backward(l, rows):
+        @pl.when(l > 0)
+        def _():
+            scan(lax.rem(l + 2, LOWER), 1, far_scan, rows, half * span)
+
     @functools.partial(each, LOWER)
     def _(l):
-        each(chains, lambda ch: relay_column(l, ch))
+        early(lambda ch: relay_column(l, ch))
+
+        @pl.when(l == 0)
+        def _():
+            late(lambda ch: spread_column(0, ch))
+
+        @pl.when(l > 0)
+        def _():
+            late(lambda ch: next_forward(lax.rem(l + 2, LOWER), ch))
+
         load_blk(l).wait()
-        each(chains, lambda ch: near_forward(l, ch))
-
-        @pl.when(l < 2)
-        def _():
-            far_forward(l)
-
-        each(chains, lambda ch: next_forward(l, ch))
+        early(lambda ch: near_forward(l, ch))
+        late(lambda ch: relay_column(l, ch))
+        far_forward(l, early_rows)
+        early(lambda ch: next_forward(l, ch))
+        late(lambda ch: near_forward(l, ch))
+        far_forward(l, late_rows)
 
     @functools.partial(each, LOWER)
     def _(step):
         l = 2 - step
-        each(chains, lambda ch: near_backward(l, ch))
-
-        @pl.when(l > 0)
-        def _():
-            scan(lax.rem(l + 2, LOWER), 1, far_scan, slice(None), N)
-
+        early(lambda ch: near_backward(l, ch))
+
+        @pl.when(l == 2)
+        def _():
+            late(lambda ch: next_forward(2, ch))
+
+        @pl.when(l < 2)
+        def _():
+            late(lambda ch: next_backward(lax.rem(l + 1, LOWER), ch))
+
+        early(lambda ch: relay_backward(l, ch))
+        late(lambda ch: near_backward(l, ch))
+        far_backward(l, early_rows)
+        early(lambda ch: next_backward(l, ch))
+        late(lambda ch: relay_backward(l, ch))
+        far_backward(l, late_rows)
         sol_out[l + 1] = sol_t[l + 1].T.astype(BF16)
         back_out[l + 1] = back_t[l + 1].T
-        each(chains, lambda ch: relay_backward(l, ch))
-        each(chains, lambda ch: next_backward(l, ch))
-
+
+    late(lambda ch: next_backward(0, ch))
     sol_out[0] = sol_t[0].T.astype(BF16)
     back_out[0] = back_t[0].T
 

time: 111 us -> 109 us (0.982)
  Pallas kernels: 107 us -> 105 us
    pallas_call x1, Pallas kernels: 107 us -> 105 us  [body(): pl.pallas_call(run, out_shape=(jax.ShapeDtypeStruct((LEVELS, N, N), BF16)...]
where the time goes in v3:
time: 109 us
  Pallas kernels  105 us (96%)
  local copies, waits for them, and re-layouts  3.24 us (3%)
    pallas_call x1, Pallas kernels, body(): pl.pallas_call(run, out_shape=(jax.ShapeDtypeStruct((LEVELS, N, N), BF16)...  105 us
    unnamed x2, local copies, waits for them, and re-layouts  3.24 us

profile of v3, /device:TPU:1, one launch (start us, length us, event | category | flops | bytes accessed | tf_op | source)
XLA Modules:
  0.0 109.1 jit_solution(15051853777108810526)
XLA Ops:
  0.6 105.2 %shard_map.59 = (bf16[4,128,128]{2,1,0:T(8,128)(2,1)}, f32[4,128,128]{2,1,0:T(8,128)}) custom-call(s32[3,6,2,8]{3,2,1,0:T(2,128)} %bitcast.17, f32[4,128,128]{2,1,0:T(8,128)} %bitcast.13, bf16[4,128,128]{2,1,0:T(8,128)(2,1)} %bitcast.15, bf16[3,96,128,128]{3,2,1,0:T(8,128)(2,1)} %bitcast.12), custom_call_target="tpu_custom_call" | custom-call | tf_op jit(solution)/shard_map/pallas_call | solution.py:426
  105.9 1.6 %copy.10 = bf16[4,1,1,128,128]{4,3,2,1,0:T(8,128)(2,1)} copy(bf16[4,1,1,128,128]{4,3,2,1,0:T(8,128)(2,1)} %bitcast.16) | data formatting | bytes 262144
  107.4 1.7 %copy.11 = f32[4,1,1,128,128]{4,3,2,1,0:T(8,128)} copy(f32[4,1,1,128,128]{4,3,2,1,0:T(8,128)} %bitcast.14) | data formatting | bytes 524288

commit v4 on v3

--- a/solution.py
+++ b/solution.py
@@ -70,8 +70,8 @@
         float_table[1, lh:lh + 1, :] = jnp.where(down(a == column, 1) > 0, 1.0, 0.0)
 
 
-def kernel(span, src, rs_hbm, inv_hbm, blk_hbm, sol_out, back_out,
-           rs, inv, rs_t, sol_t, back_t, blk, gathered, part_out, part_in, copies, seg, ry, rz, s2, s3,
+def kernel(span, src, rs_hbm, inv_hbm, blk_hbm, sol_t, back_t,
+           rs, inv, rs_t, blk, gathered, part_out, part_in, copies, seg, ry, rz, s2, s3,
            fz, fy, pending, held, held_back, near_scan, far_scan,
            int_vec, float_vec, ints, floats, in_sem, z_sem, f_sem, b_sem):
     chains = N // span
@@ -377,12 +377,8 @@
         early(lambda ch: next_backward(l, ch))
         late(lambda ch: relay_backward(l, ch))
         far_backward(l, late_rows)
-        sol_out[l + 1] = sol_t[l + 1].T.astype(BF16)
-        back_out[l + 1] = back_t[l + 1].T
 
     late(lambda ch: next_backward(0, ch))
-    sol_out[0] = sol_t[0].T.astype(BF16)
-    back_out[0] = back_t[0].T
 
     @functools.partial(each, LOWER * chains)
     def _(k):
@@ -393,6 +389,12 @@
         wait_for(gathered.at[l, ch, pl.ds(0, 31)], b_sem.at[k, 2])
 
 
+def turn(sol_t, back_t, sol_out, back_out):
+    for level in range(LEVELS):
+        sol_out[level] = sol_t[level].T.astype(BF16)
+        back_out[level] = back_t[level].T
+
+
 def body(right_sides, inverses, blocks, sources):
     chains = CHAINS
     span = N // chains
@@ -404,7 +406,7 @@
         return pltpu.VMEM((*lead, N, N), dtype)
 
     scratch = [
-        whole(LEVELS), whole(LEVELS, dtype=BF16), whole(LEVELS), whole(LEVELS), whole(LEVELS),
+        whole(LEVELS), whole(LEVELS, dtype=BF16), whole(LEVELS),
         whole(LOWER, 2 * HALF, dtype=BF16),
         tile(COLS), tile(ROWS), tile(ROWS - 1), tile(ROWS),
         tile(DEEP, WIDE), tile(3, 5), tile(2, WIDE), tile(5), tile(3), tile(5), tile(3),
@@ -426,7 +428,7 @@
     solved, back = pl.pallas_call(
         run,
         out_shape=(
-            jax.ShapeDtypeStruct((LEVELS, N, N), BF16),
+            jax.ShapeDtypeStruct((LEVELS, N, N), F32),
             jax.ShapeDtypeStruct((LEVELS, N, N), F32),
         ),
         in_specs=[smem] + [hbm] * 3,
@@ -437,6 +439,15 @@
         ),
     )(jnp.transpose(sources[:, 0, 0], (0, 3, 1, 2)), right_sides[:, 0, 0], inverses[:, 0, 0],
       blocks[:, 0, 0].reshape(LOWER, 2 * HALF, N, N))
+    solved, back = pl.pallas_call(
+        turn,
+        out_shape=(
+            jax.ShapeDtypeStruct((LEVELS, N, N), BF16),
+            jax.ShapeDtypeStruct((LEVELS, N, N), F32),
+        ),
+        in_specs=[vmem, vmem],
+        out_specs=(vmem, vmem),
+    )(solved, back)
     return solved[:, None, None], back[:, None, None]
 
 

time: 109 us -> 109 us (level)
  local copies, waits for them, and re-layouts: 3.24 us -> 0 us
  Pallas kernels: 105 us -> 108 us
    unnamed x2 -> x0, local copies, waits for them, and re-layouts: 3.24 us -> none
    pallas_call x1 -> x2, Pallas kernels: 105 us -> 108 us  [the longest x1 106 us: body(): pl.pallas_call(run, out_shape=(jax.ShapeDtypeStruct((LEVELS, N, N), F32),...]
where the time goes in v4:
time: 109 us
  Pallas kernels  108 us (99%)
    pallas_call x1, Pallas kernels, body(): pl.pallas_call(run, out_shape=(jax.ShapeDtypeStruct((LEVELS, N, N), F32),...  106 us

profile of v4, /device:TPU:1, one launch (start us, length us, event | category | flops | bytes accessed | tf_op | source)
XLA Modules:
  0.0 108.8 jit_solution(9924535238632827644)
XLA Ops:
  0.6 106.2 %shard_map.59 = (f32[4,128,128]{2,1,0:T(8,128)}, f32[4,128,128]{2,1,0:T(8,128)}) custom-call(s32[3,6,2,8]{3,2,1,0:T(2,128)} %bitcast.15, f32[4,128,128]{2,1,0:T(8,128)} %bitcast.13, bf16[4,128,128]{2,1,0:T(8,128)(2,1)} %bitcast.14, bf16[3,96,128,128]{3,2,1,0:T(8,128)(2,1)} %bitcast.12), custom_call_target="tpu_custom_call" | custom-call | tf_op jit(solution)/shard_map/pallas_call | solution.py:428
  106.9 1.9 %shard_map.60 = (bf16[4,128,128]{2,1,0:T(8,128)(2,1)}, f32[4,128,128]{2,1,0:T(8,128)}) custom-call(f32[4,128,128]{2,1,0:T(8,128)} %get-tuple-element.6.sol_t, f32[4,128,128]{2,1,0:T(8,128)} %get-tuple-element.7.back_t), custom_call_target="tpu_custom_call" | custom-call | tf_op jit(solution)/shard_map/pallas_call | solution.py:442
